TPU v7x, 32 devices: a whole 2x2x4 slice. The times are simulated.
32 devices in a mesh: groups: 2 (over y), row: 4 (over z), col: 4 (over x, core).
Axes of the slice: x: 2, y: 2, z: 4, core: 2. Of those that a mesh axis runs over, the one named last changes fastest.
Arguments:
- grad_out: bfloat16 [2048, 12288], P(('groups', 'row'), 'col'), parts along dimension 0, may hold values from -6 to 6
- preact: bfloat16 [2048, 24576], P(('groups', 'col'), 'row'), parts along dimension 0, may hold values from -6 to 6
- down_weight: bfloat16 [24576, 12288], P('row', 'col'), may hold values from -0.0546875 to 0.0546875
- sketch_matrix: bfloat16 [24576, 512], P('row'), may hold values from -0.0017089844 to 0.0017089844
Outputs:
- grad_pre: bfloat16 [2048, 24576], P(('groups', 'col'), 'row'), parts along dimension 0
- sketch: float32 [1024, 12288], P(('groups', 'row'), 'col'), parts along dimension 0
There are 2 independent parts, one for each index of `groups`. A program takes and returns all parts, laid end to end along the dimension named above; an argument that names none is the same for every part. Nothing has to cross between parts.
All inputs are finite; a program needn't handle non-finite values.
Results may differ from a plain program's by a relative error of at most 0.011.
Values may be sent and summed in bfloat16 or wider, within the bound.
A program may use at most 192 MiB of HBM per device.

v0:
```python
import jax
import jax.numpy as jnp
from jax import lax
from jax.sharding import PartitionSpec as P

gelu_scale = 0.7978845608028654
cubic_term = 0.044715


def gelu_parts(preact):
    pre_f32 = preact.astype(jnp.float32)
    inner_arg = gelu_scale * (pre_f32 + cubic_term * pre_f32 * pre_f32 * pre_f32)
    tangent = jnp.tanh(inner_arg)
    value = 0.5 * pre_f32 * (1.0 + tangent)
    slope = 0.5 * (1.0 + tangent) + 0.5 * pre_f32 * (1.0 - tangent * tangent) * gelu_scale * (
        1.0 + 3.0 * cubic_term * pre_f32 * pre_f32
    )
    return (value, slope)


def per_device(grad_out, preact, down_weight, sketch_matrix):
    grad_rows = lax.all_gather(grad_out, "row", axis=0, tiled=True)
    hidden_grad = lax.psum_scatter(
        lax.dot_general(
            grad_rows, down_weight, (((1,), (1,)), ((), ())), preferred_element_type=jnp.float32
        ).astype(jnp.bfloat16),
        "col",
        scatter_dimension=0,
        tiled=True,
    ).astype(jnp.float32)
    value, slope = gelu_parts(preact)
    grad_pre = (hidden_grad * slope).astype(jnp.bfloat16)
    act_local = value.astype(jnp.bfloat16)
    act_every = lax.all_gather(act_local, "col", axis=0, tiled=True)
    reduced = lax.psum_scatter(
        lax.dot_general(
            sketch_matrix, act_every, (((0,), (1,)), ((), ())), preferred_element_type=jnp.float32
        ).astype(jnp.bfloat16),
        "row",
        scatter_dimension=0,
        tiled=True,
    ).astype(jnp.float32)
    sketch = jnp.dot(
        reduced,
        grad_rows.astype(jnp.float32),
        precision=lax.Precision.HIGHEST,
        preferred_element_type=jnp.float32,
    )
    return (grad_pre, sketch)


def solution(mesh):
    in_specs = (
        P(("groups", "row"), "col"),
        P(("groups", "col"), "row"),
        P("row", "col"),
        P("row", None),
    )
    out_specs = (P(("groups", "col"), "row"), P(("groups", "row"), "col"))
    return jax.shard_map(
        per_device, mesh=mesh, in_specs=in_specs, out_specs=out_specs, check_vma=False
    )
```

profile of v0, /device:TPU:0, one launch (start us, length us, event | category | flops | bytes accessed | tf_op | source)
XLA Modules:
  0.0 413.0 jit_solution(18400250298376004255)
XLA Ops:
  7.2 0.0 all-gather.3.cloned.1.call-start
  7.2 0.7 all-gather.3.cloned.1.call-update
  7.9 0.0 reduce-scatter.5.cloned.1.call-start
  7.9 119.7 %all-gather.3.cloned.1.call-done = bf16[1024,3072]{1,0:T(8,128)(2,1)} async-done(((bf16[256,3072]{1,0:T(8,128)(2,1)}), bf16[1024,3072]{1,0:T(8,128)(2,1)}) %all-gather.3.cloned.1.call-update) | async-done | bytes 6291472 | tf_op jit(solution)/shard_map/all_gather | solution.py:22
  127.7 46.2 %convolution_convert_fusion = bf16[1024,6144]{1,0:T(8,128)(2,1)} fusion(bf16[1024,3072]{1,0:T(8,128)(2,1)} %all-gather.3.cloned.1.call-done, bf16[6144,3072]{1,0:T(8,128)(2,1)} %param.6), kind=kOutput, calls=%fused_computation.7 | convolution fusion | flops 38660997120 | bytes 56623104 | tf_op jit(solution)/shard_map/dot_general | solution.py:24
  173.8 0.0 copy-start
  173.8 0.0 reduce-scatter.5.cloned.1.call-update
  173.8 0.0 all-gather.5.cloned.1.call-start
  173.9 97.4 %reduce-scatter.5.cloned.1.call-done = bf16[256,6144]{1,0:T(8,128)(2,1)} async-done(((bf16[1024,6144]{1,0:T(8,128)(2,1)}), bf16[256,6144]{1,0:T(8,128)(2,1)}) %reduce-scatter.5.cloned.1.call-update) | async-done | bytes 3145744 | tf_op jit(solution)/shard_map/reduce_scatter | solution.py:23
  271.3 0.0 copy-done
  271.3 7.8 %fusion.7 = (bf16[256,6144]{1,0:T(8,128)(2,1)}, bf16[256,6144]{1,0:T(8,128)(2,1)}) fusion(bf16[256,6144]{1,0:T(8,128)(2,1)S(1)} %copy-done, bf16[256,6144]{1,0:T(8,128)(2,1)} %reduce-scatter.5.cloned.1.call-done), kind=kLoop, calls=%fused_computation.15 | loop fusion | flops 36175872 | bytes 12582912 | tf_op jit(solution)/shard_map/convert_element_type | solution.py:33
  279.1 0.0 all-gather.5.cloned.1.call-update
  279.1 0.0 reduce-scatter.7.cloned.1.call-start
  279.1 82.2 %all-gather.5.cloned.1.call-done = bf16[1024,6144]{1,0:T(8,128)(2,1)} async-done(((bf16[256,6144]{1,0:T(8,128)(2,1)}), bf16[1024,6144]{1,0:T(8,128)(2,1)}) %all-gather.5.cloned.1.call-update) | async-done | bytes 12582928 | tf_op jit(solution)/shard_map/all_gather | solution.py:34
  361.3 11.4 %fusion.11 = bf16[512,1024]{0,1:T(8,128)(2,1)S(1)} fusion(bf16[1024,6144]{1,0:T(8,128)(2,1)} %all-gather.5.cloned.1.call-done, bf16[6144,512]{1,0:T(8,128)(2,1)} %param.7), kind=kOutput, calls=%fused_computation.20 | convolution fusion | flops 6442975232 | bytes 19922944 | tf_op jit(solution)/shard_map/dot_general | solution.py:36
  372.8 1.3 copy.6
  374.1 0.0 reduce-scatter.7.cloned.1.call-update
  374.1 27.3 %reduce-scatter.7.cloned.1.call-done = bf16[128,1024]{1,0:T(8,128)(2,1)} async-done(((bf16[512,1024]{1,0:T(8,128)(2,1)}), bf16[128,1024]{1,0:T(8,128)(2,1)}) %reduce-scatter.7.cloned.1.call-update) | async-done | bytes 262160
  401.4 5.0 %fusion.12 = f32[128,3072]{1,0:T(8,128)} fusion(bf16[128,1024]{1,0:T(8,128)(2,1)} %reduce-scatter.7.cloned.1.call-done, bf16[1024,3072]{1,0:T(8,128)(2,1)} %all-gather.3.cloned.1.call-done), kind=kOutput, calls=%fused_computation.21 | convolution fusion | flops 805306368 | bytes 8126464 | tf_op jit(solution)/shard_map/dot_general | solution.py:43
Async XLA Ops:
  7.2 120.5 %all-gather.3.cloned.1.call-start = ((), (), s32[]{:S(2)}) async-start(), calls=%async_computation.2 | async-start | bytes 7864320 | tf_op jit(solution)/shard_map/all_gather | solution.py:22
  7.9 263.4 %reduce-scatter.5.cloned.1.call-start = ((), (), s32[]{:S(2)}) async-start(), calls=%async_computation.3 | async-start | bytes 15728640 | tf_op jit(solution)/shard_map/reduce_scatter | solution.py:23
  173.8 97.5 %copy-start = (bf16[256,6144]{1,0:T(8,128)(2,1)S(1)}, bf16[256,6144]{1,0:T(8,128)(2,1)}, u32[]{:S(2)}) copy-start(bf16[256,6144]{1,0:T(8,128)(2,1)} %param.5) | copy-start | bytes 9437188
  173.8 187.5 %all-gather.5.cloned.1.call-start = ((), (), s32[]{:S(2)}) async-start(), calls=%async_computation.4 | async-start | bytes 15728640 | tf_op jit(solution)/shard_map/all_gather | solution.py:34
  279.1 122.4 %reduce-scatter.7.cloned.1.call-start = ((), (), s32[]{:S(2)}) async-start(), calls=%async_computation.5 | async-start | bytes 1310720
Sparse Core Ops, SparseCore 0:
  9.6 118.0 all-gather.2
  174.0 97.2 reduce-scatter.4
  279.2 82.1 all-gather.4
  374.3 27.1 reduce-scatter.6
where the time goes:
time: 413 us
  waiting for transfers between devices  327 us (79%)
  matrix products  62.6 us (15%)
  between operations  13.8 us (3%)
  other arithmetic  7.78 us (2%)
    all_gather x1, waiting for transfers between devices, per_device(): grad_rows = lax.all_gather(grad_out, 'row', axis=0, tiled=True)  120 us
    reduce_scatter x1, waiting for transfers between devices, per_device(): lax.psum_scatter(lax.dot_general(grad_rows, down_weight, (((1,), (1,)), (...  97.4 us
    all_gather x1, waiting for transfers between devices, per_device(): act_every = lax.all_gather(act_local, 'col', axis=0, tiled=True)  82.2 us
    dot_general x1, matrix products, per_device(): lax.dot_general(grad_rows, down_weight, (((1,), (1,)), ((), ())), preferr...  46.2 us
    unnamed x5, waiting for transfers between devices  28 us
    dot_general x1, matrix products, per_device(): lax.dot_general(sketch_matrix, act_every, (((0,), (1,)), ((), ())), prefe...  11.4 us
  transfers between devices with their start and end apart: 4, of which 4 were waited for; matrix products, arithmetic and copies ran while one was open for 0% of the time, Pallas kernels for 0%

commit v1 on v0

--- a/solution.py
+++ b/solution.py
@@ -20,6 +20,13 @@
 
 def per_device(grad_out, preact, down_weight, sketch_matrix):
     grad_rows = lax.all_gather(grad_out, "row", axis=0, tiled=True)
+    value, slope = gelu_parts(preact)
+    act_local = value.astype(jnp.bfloat16)
+    own = lax.dot_general(
+        sketch_matrix, act_local, (((0,), (1,)), ((), ())), preferred_element_type=jnp.float32
+    )
+    reduced = lax.psum_scatter(own, "row", scatter_dimension=0, tiled=True)
+    reduced = lax.all_gather(reduced.astype(jnp.bfloat16), "col", axis=1, tiled=True)
     hidden_grad = lax.psum_scatter(
         lax.dot_general(
             grad_rows, down_weight, (((1,), (1,)), ((), ())), preferred_element_type=jnp.float32
@@ -28,24 +35,8 @@
         scatter_dimension=0,
         tiled=True,
     ).astype(jnp.float32)
-    value, slope = gelu_parts(preact)
     grad_pre = (hidden_grad * slope).astype(jnp.bfloat16)
-    act_local = value.astype(jnp.bfloat16)
-    act_every = lax.all_gather(act_local, "col", axis=0, tiled=True)
-    reduced = lax.psum_scatter(
-        lax.dot_general(
-            sketch_matrix, act_every, (((0,), (1,)), ((), ())), preferred_element_type=jnp.float32
-        ).astype(jnp.bfloat16),
-        "row",
-        scatter_dimension=0,
-        tiled=True,
-    ).astype(jnp.float32)
-    sketch = jnp.dot(
-        reduced,
-        grad_rows.astype(jnp.float32),
-        precision=lax.Precision.HIGHEST,
-        preferred_element_type=jnp.float32,
-    )
+    sketch = jnp.dot(reduced, grad_rows, preferred_element_type=jnp.float32)
     return (grad_pre, sketch)
 
 

time: 413 us -> 285 us (0.69)
  waiting for transfers between devices: 327 us -> 198 us
  blocking collectives: 0 us -> 5.77 us
    all_gather x1 -> x0, waiting for transfers between devices: 82.2 us -> none  [per_device(): act_every = lax.all_gather(act_local, 'col', axis=0, tiled=True)]
    unnamed x5 -> x3, waiting for transfers between devices: 28 us -> 0.71 us
    reduce_scatter x1, waiting for transfers between devices: 97.4 us -> 84.1 us  [per_device(): lax.psum_scatter(lax.dot_general(grad_rows, down_weight, (((1,), (1,)), (...]
    all_gather x1, waiting for transfers between devices: 120 us -> 113 us  [per_device(): grad_rows = lax.all_gather(grad_out, 'row', axis=0, tiled=True)]
    all_gather x0 -> x1, blocking collectives: none -> 5.77 us  [per_device(): lax.all_gather(reduced.astype(jnp.bfloat16), 'col', axis=1, tiled=True)]
  transfers between devices with their start and end apart: 4 -> 3, of which waited for: 4 -> 2; matrix products, arithmetic and copies ran while one was open for 0% -> 21% of each run, Pallas kernels for 0% -> 0%
where the time goes in v1:
time: 285 us
  waiting for transfers between devices  198 us (69%)
  matrix products  59.7 us (21%)
  between operations  13.8 us (5%)
  other arithmetic  7.84 us (3%)
  blocking collectives  5.77 us (2%)
    all_gather x1, waiting for transfers between devices, per_device(): grad_rows = lax.all_gather(grad_out, 'row', axis=0, tiled=True)  113 us
    reduce_scatter x1, waiting for transfers between devices, per_device(): lax.psum_scatter(lax.dot_general(grad_rows, down_weight, (((1,), (1,)), (...  84.1 us
    dot_general x1, matrix products, per_device(): lax.dot_general(grad_rows, down_weight, (((1,), (1,)), ((), ())), preferr...  46.2 us
    convert_element_type x1, other arithmetic, per_device(): grad_pre = (hidden_grad * slope).astype(jnp.bfloat16)  6.93 us
    dot_general x1, matrix products, per_device(): lax.dot_general(sketch_matrix, act_local, (((0,), (1,)), ((), ())), prefe...  6.89 us
    dot_general x1, matrix products, per_device(): sketch = jnp.dot(reduced, grad_rows, preferred_element_type=jnp.float32)  6.62 us
    all_gather x1, blocking collectives, per_device(): lax.all_gather(reduced.astype(jnp.bfloat16), 'col', axis=1, tiled=True)  5.77 us
  transfers between devices with their start and end apart: 3, of which 2 were waited for; matrix products, arithmetic and copies ran while one was open for 21% of the time, Pallas kernels for 0%

profile of v1, /device:TPU:0, one launch (start us, length us, event | category | flops | bytes accessed | tf_op | source)
XLA Modules:
  0.0 284.8 jit_solution(17811838550323162167)
XLA Ops:
  7.2 0.0 all-gather.2.cloned.1.call-start
  7.2 0.7 all-gather.2.cloned.1.call-update
  7.9 0.0 reduce-scatter.5.cloned.1.call-start
  7.9 6.9 %fusion.13 = f32[512,256]{0,1:T(8,128)} fusion(bf16[6144,512]{1,0:T(8,128)(2,1)} %param.7, bf16[256,6144]{1,0:T(8,128)(2,1)} %param.5), kind=kOutput, calls=%fused_computation.20 | convolution fusion | flops 1626341376 | bytes 9961472 | tf_op jit(solution)/shard_map/dot_general | solution.py:25
  14.8 0.0 reduce-scatter.5.cloned.1.call-update
  14.9 0.0 reduce-scatter.3.cloned.1.call-start
  14.9 112.7 %all-gather.2.cloned.1.call-done = bf16[1024,3072]{1,0:T(8,128)(2,1)} async-done(((bf16[256,3072]{1,0:T(8,128)(2,1)}), bf16[1024,3072]{1,0:T(8,128)(2,1)}) %all-gather.2.cloned.1.call-update) | async-done | bytes 6291472 | tf_op jit(solution)/shard_map/all_gather | solution.py:22
  127.7 46.2 %convolution_convert_fusion = bf16[1024,6144]{1,0:T(8,128)(2,1)} fusion(bf16[1024,3072]{1,0:T(8,128)(2,1)} %all-gather.2.cloned.1.call-done, bf16[6144,3072]{1,0:T(8,128)(2,1)} %param.6), kind=kOutput, calls=%fused_computation.7 | convolution fusion | flops 38660997120 | bytes 56623104 | tf_op jit(solution)/shard_map/dot_general | solution.py:31
  173.8 0.0 reduce-scatter.3.cloned.1.call-update
  173.9 0.0 reduce-scatter.5.cloned.1.call-done
  173.9 0.9 convert_element_type.23
  174.8 5.8 %all_gather.7 = bf16[128,1024]{0,1:T(8,128)(2,1)S(1)} all-gather(bf16[128,256]{0,1:T(8,128)(2,1)S(1)} %convert_element_type.23), channel_id=1, replica_groups=mesh['groups'=2,'row'=4,'col'=4] {'col'}, dimensions={1}, use_global_device_ids=true | all-gather | bytes 327680 | tf_op jit(solution)/shard_map/all_gather | solution.py:29
  180.6 0.0 copy-start
  180.6 6.6 %fusion.20 = f32[128,3072]{1,0:T(8,128)} fusion(bf16[128,1024]{0,1:T(8,128)(2,1)S(1)} %all_gather.7, bf16[1024,3072]{1,0:T(8,128)(2,1)} %all-gather.2.cloned.1.call-done), kind=kOutput, calls=%fused_computation.25 | convolution fusion | flops 805306368 | bytes 8126464 | tf_op jit(solution)/shard_map/dot_general | solution.py:39
  187.2 84.1 %reduce-scatter.3.cloned.1.call-done = bf16[256,6144]{1,0:T(8,128)(2,1)} async-done(((bf16[1024,6144]{1,0:T(8,128)(2,1)}), bf16[256,6144]{1,0:T(8,128)(2,1)}) %reduce-scatter.3.cloned.1.call-update) | async-done | bytes 3145744 | tf_op jit(solution)/shard_map/reduce_scatter | solution.py:30
  271.3 0.0 copy-done
  271.3 6.9 %fusion.6 = bf16[256,6144]{1,0:T(8,128)(2,1)} fusion(bf16[256,6144]{1,0:T(8,128)(2,1)S(1)} %copy-done, bf16[256,6144]{1,0:T(8,128)(2,1)} %reduce-scatter.3.cloned.1.call-done), kind=kLoop, calls=%fused_computation.14 | loop fusion | flops 33030144 | bytes 9437184 | tf_op jit(solution)/shard_map/convert_element_type | solution.py:38
Async XLA Ops:
  7.2 120.5 %all-gather.2.cloned.1.call-start = ((), (), s32[]{:S(2)}) async-start(), calls=%async_computation.2 | async-start | bytes 7864320 | tf_op jit(solution)/shard_map/all_gather | solution.py:22
  7.9 166.0 %reduce-scatter.5.cloned.1.call-start = ((), (), s32[]{:S(2)}) async-start(), calls=%async_computation.4 | async-start | bytes 655360 | tf_op jit(solution)/shard_map/reduce_scatter | solution.py:28
  14.9 256.4 %reduce-scatter.3.cloned.1.call-start = ((), (), s32[]{:S(2)}) async-start(), calls=%async_computation.3 | async-start | bytes 15728640 | tf_op jit(solution)/shard_map/reduce_scatter | solution.py:30
  180.6 90.7 %copy-start = (bf16[256,6144]{1,0:T(8,128)(2,1)S(1)}, bf16[256,6144]{1,0:T(8,128)(2,1)}, u32[]{:S(2)}) copy-start(bf16[256,6144]{1,0:T(8,128)(2,1)} %param.5) | copy-start | bytes 9437188
Sparse Core Ops, SparseCore 0:
  9.6 118.0 all-gather.1
  130.5 19.8 reduce-scatter.4
  174.0 97.2 reduce-scatter.2

commit v2 on v1

--- a/solution.py
+++ b/solution.py
@@ -1,6 +1,8 @@
 import jax
 import jax.numpy as jnp
 from jax import lax
+from jax.experimental import pallas as pl
+from jax.experimental.pallas import tpu as pltpu
 from jax.sharding import PartitionSpec as P
 
 gelu_scale = 0.7978845608028654
@@ -40,7 +42,324 @@
     return (grad_pre, sketch)
 
 
+MESH = pl.DeviceIdType.MESH
+LINE = 4
+TILES = 6
+
+
+def fits(mesh):
+    return mesh.shape["row"] == LINE and mesh.shape["col"] == LINE
+
+
+def pick(index, options):
+    chosen = options[0]
+    for place, option in enumerate(options[1:], 1):
+        chosen = jnp.where(index == place, option, chosen)
+    return chosen
+
+
+def encoded(pieces):
+    code = 0
+    for piece in reversed(pieces):
+        code = code * 8 + piece
+    return code
+
+
+def arrival_orders():
+    orders = []
+    for place in range(LINE):
+        order = [2 * place, 2 * place + 1]
+        for distance in range(1, LINE):
+            for half in range(2):
+                for other in (place - distance, place + distance):
+                    if 0 <= other < LINE:
+                        order.append(2 * other + half)
+        orders.append(encoded(order))
+    return orders
+
+
+def kernel(
+    g_ref, w_ref, slope_ref, out_ref, rows_ref,
+    wbuf, gbuf, pbuf, near, far, sums, slopes,
+    w_sem, g_sem, own_sem, slope_sem, out_sem, right_sem, left_sem, got_sem,
+    near_send, near_got, far_send, far_got, sum_send, sum_got,
+):
+    z = lax.axis_index("row")
+    c = lax.axis_index("col")
+    par = lax.rem(c, 2)
+    other = 1 - par
+    partner = c + 1 - 2 * par
+    chip = lax.div(c, 2)
+    has_left, has_right = z > 0, z < LINE - 1
+    piece_rows = gbuf.shape[0]
+    tile = wbuf.shape[2]
+    half_width = tile * TILES
+
+    def w_copy(half, j):
+        start = pl.multiple_of((half * TILES + j) * tile, tile)
+        return pltpu.make_async_copy(w_ref.at[pl.ds(start, tile)], wbuf.at[half, j], w_sem.at[half, j])
+
+    def slope_copy(h, half):
+        return pltpu.make_async_copy(
+            slope_ref.at[pl.ds(h * piece_rows, piece_rows), pl.ds(half * half_width, half_width)],
+            slopes.at[h, half],
+            slope_sem.at[h, half],
+        )
+
+    def out_copy(h, half):
+        return pltpu.make_async_copy(
+            pbuf.at[2 * c + h, half],
+            out_ref.at[pl.ds(h * piece_rows, piece_rows), pl.ds(half * half_width, half_width)],
+            out_sem.at[h, half],
+        )
+
+    def rows_of(piece):
+        return rows_ref.at[pl.ds(pl.multiple_of(piece * piece_rows, piece_rows), piece_rows)]
+
+    def own_copy():
+        return pltpu.make_async_copy(
+            g_ref, rows_ref.at[pl.ds(pl.multiple_of(z * 2 * piece_rows, 2 * piece_rows), 2 * piece_rows)], own_sem
+        )
+
+    def pass_on(piece, step, sem, source):
+        return pltpu.make_async_remote_copy(
+            src_ref=source, dst_ref=rows_of(piece), send_sem=sem.at[piece], recv_sem=got_sem.at[piece],
+            device_id={"row": z + step}, device_id_type=MESH,
+        )
+
+    def near_copy(piece, h, half):
+        return pltpu.make_async_remote_copy(
+            src_ref=pbuf.at[piece, half], dst_ref=near.at[h, half],
+            send_sem=near_send.at[h, half], recv_sem=near_got.at[h, half],
+            device_id={"col": partner}, device_id_type=MESH,
+        )
+
+    def far_copy(piece, index):
+        return pltpu.make_async_remote_copy(
+            src_ref=pbuf.at[piece, other], dst_ref=far.at[index],
+            send_sem=far_send.at[index], recv_sem=far_got.at[index],
+            device_id={"col": partner}, device_id_type=MESH,
+        )
+
+    def sum_copy(piece, owner, h, half, index):
+        return pltpu.make_async_remote_copy(
+            src_ref=pbuf.at[piece, half], dst_ref=sums.at[h, half],
+            send_sem=sum_send.at[index], recv_sem=sum_got.at[h, half],
+            device_id={"col": owner}, device_id_type=MESH,
+        )
+
+    own_copy().start()
+
+    @pl.loop(0, TILES)
+    def _(j):
+        w_copy(other, j).start()
+
+    barrier = pltpu.get_barrier_semaphore()
+    for step in range(1, LINE):
+        pl.semaphore_signal(barrier, inc=1, device_id={"col": lax.rem(c + step, LINE)}, device_id_type=MESH)
+
+    @pl.when(has_left)
+    def _():
+        pl.semaphore_signal(barrier, inc=1, device_id={"row": z - 1}, device_id_type=MESH)
+
+    @pl.when(has_right)
+    def _():
+        pl.semaphore_signal(barrier, inc=1, device_id={"row": z + 1}, device_id_type=MESH)
+
+    pl.semaphore_wait(barrier, LINE - 1 + jnp.where(has_left, 1, 0) + jnp.where(has_right, 1, 0))
+
+    for h in range(2):
+        source = g_ref.at[pl.ds(h * piece_rows, piece_rows)]
+
+        @pl.when(has_left)
+        def _():
+            pass_on(2 * z + h, -1, left_sem, source).start()
+
+        @pl.when(has_right)
+        def _():
+            pass_on(2 * z + h, 1, right_sem, source).start()
+
+    @pl.loop(0, TILES)
+    def _(j):
+        w_copy(par, j).start()
+
+    for h in range(2):
+        for half in range(2):
+            slope_copy(h, half).start()
+    own_copy().wait()
+
+    def step_of(s, code):
+        piece = lax.rem(code, 8)
+        owner = lax.div(piece, 2)
+        h = lax.rem(piece, 2)
+        is_near = owner == partner
+        is_far = lax.div(owner, 2) != chip
+        index = 2 * lax.rem(owner, 2) + h
+
+        @pl.when(owner != z)
+        def _():
+            pass_on(piece, 0, left_sem, rows_of(piece)).wait_recv()
+
+        @pl.when((owner < z) & has_right)
+        def _():
+            pass_on(piece, 1, right_sem, rows_of(piece)).start()
+
+        @pl.when((owner > z) & has_left)
+        def _():
+            pass_on(piece, -1, left_sem, rows_of(piece)).start()
+
+        load = pltpu.make_async_copy(rows_of(piece), gbuf, g_sem)
+        load.start()
+        load.wait()
+
+        def multiply(half):
+            @pl.loop(0, TILES)
+            def _(j):
+                @pl.when(s == 0)
+                def _():
+                    w_copy(half, j).wait()
+
+                product = lax.dot_general(
+                    gbuf[...], wbuf[half, j], (((1,), (1,)), ((), ())), preferred_element_type=jnp.float32
+                )
+                pbuf[piece, half, :, pl.ds(pl.multiple_of(j * tile, tile), tile)] = product.astype(jnp.bfloat16)
+
+        multiply(other)
+
+        @pl.when(is_near)
+        def _():
+            near_copy(piece, h, other).start()
+
+        @pl.when(is_far)
+        def _():
+            far_copy(piece, index).start()
+
+        multiply(par)
+
+        @pl.when(is_near)
+        def _():
+            near_copy(piece, h, par).start()
+
+        @pl.when(is_far)
+        def _():
+            far_copy(piece, index).wait_recv()
+
+            @pl.loop(0, TILES)
+            def _(j):
+                columns = pl.ds(pl.multiple_of(j * tile, tile), tile)
+                total = pbuf[piece, par, :, columns].astype(jnp.float32) + far[index, :, columns].astype(jnp.float32)
+                pbuf[piece, par, :, columns] = total.astype(jnp.bfloat16)
+
+            sum_copy(piece, owner, h, par, index).start()
+
+        return lax.div(code, 8)
+
+    lax.fori_loop(0, 2 * LINE, step_of, pick(z, arrival_orders()))
+
+    for h in range(2):
+        for half in range(2):
+            near_copy(2 * partner + h, h, half).wait_recv()
+            slope_copy(h, half).wait()
+            sum_copy(2 * c + h, lax.rem(c + 2, LINE), h, half, h).wait_recv()
+
+            @pl.loop(0, TILES)
+            def _(j):
+                columns = pl.ds(pl.multiple_of(j * tile, tile), tile)
+                hidden = (
+                    pbuf[2 * c + h, half, :, columns].astype(jnp.float32)
+                    + near[h, half, :, columns].astype(jnp.float32)
+                    + sums[h, half, :, columns].astype(jnp.float32)
+                )
+                scaled = hidden * slopes[h, half, :, columns].astype(jnp.float32)
+                pbuf[2 * c + h, half, :, columns] = scaled.astype(jnp.bfloat16)
+
+            out_copy(h, half).start()
+
+    def drain(piece, carry):
+        owner = lax.div(piece, 2)
+        h = lax.rem(piece, 2)
+        index = 2 * lax.rem(owner, 2) + h
+
+        @pl.when((owner <= z) & has_right)
+        def _():
+            pass_on(piece, 1, right_sem, rows_of(piece)).wait_send()
+
+        @pl.when((owner >= z) & has_left)
+        def _():
+            pass_on(piece, -1, left_sem, rows_of(piece)).wait_send()
+
+        @pl.when(owner == partner)
+        def _():
+            near_copy(piece, h, other).wait_send()
+            near_copy(piece, h, par).wait_send()
+
+        @pl.when(lax.div(owner, 2) != chip)
+        def _():
+            far_copy(piece, index).wait_send()
+            sum_copy(piece, owner, h, par, index).wait_send()
+
+        return carry
+
+    lax.fori_loop(0, 2 * LINE, drain, 0)
+    for h in range(2):
+        for half in range(2):
+            out_copy(h, half).wait()
+
+
+def gathered_product(grad_out, down_weight, slope):
+    tokens, features = grad_out.shape
+    hidden = down_weight.shape[0]
+    rows, width = tokens // 2, hidden // 2
+    kind = grad_out.dtype
+    pair = pltpu.SemaphoreType.DMA((2, 2))
+    eight = pltpu.SemaphoreType.DMA((2 * LINE,))
+    four = pltpu.SemaphoreType.DMA((4,))
+    one = pltpu.SemaphoreType.DMA
+    return pl.pallas_call(
+        kernel,
+        out_shape=(
+            jax.ShapeDtypeStruct((tokens, hidden), kind),
+            jax.ShapeDtypeStruct((tokens * LINE, features), kind),
+        ),
+        in_specs=[pl.BlockSpec(memory_space=pltpu.HBM)] * 3,
+        out_specs=(pl.BlockSpec(memory_space=pltpu.HBM),) * 2,
+        scratch_shapes=[
+            pltpu.VMEM((2, TILES, width // TILES, features), kind),
+            pltpu.VMEM((rows, features), kind),
+            pltpu.VMEM((2 * LINE, 2, rows, width), kind),
+            pltpu.VMEM((2, 2, rows, width), kind),
+            pltpu.VMEM((4, rows, width), kind),
+            pltpu.VMEM((2, 2, rows, width), kind),
+            pltpu.VMEM((2, 2, rows, width), kind),
+            pltpu.SemaphoreType.DMA((2, TILES)),
+            one, one, pair, pair, eight, eight, eight,
+            pair, pair, four, four, four, pair,
+        ],
+        compiler_params=pltpu.CompilerParams(
+            collective_id=0, has_side_effects=True, vmem_limit_bytes=63 * 1024 * 1024
+        ),
+        cost_estimate=pl.CostEstimate(
+            flops=2 * LINE * tokens * hidden * features * 3,
+            bytes_accessed=2 * (hidden * features + 12 * tokens * features),
+            transcendentals=0,
+        ),
+    )(grad_out, down_weight, slope)
+
+
+def fused_device(grad_out, preact, down_weight, sketch_matrix):
+    value, slope = gelu_parts(preact)
+    grad_pre, grad_rows = gathered_product(grad_out, down_weight, slope.astype(jnp.bfloat16))
+    own = lax.dot_general(
+        sketch_matrix, value.astype(jnp.bfloat16), (((0,), (1,)), ((), ())), preferred_element_type=jnp.float32
+    )
+    reduced = lax.psum_scatter(own.astype(jnp.bfloat16), "row", scatter_dimension=0, tiled=True)
+    reduced = lax.all_gather(reduced.astype(jnp.bfloat16), "col", axis=1, tiled=True)
+    sketch = jnp.dot(reduced, grad_rows, preferred_element_type=jnp.float32)
+    return (grad_pre, sketch)
+
+
 def solution(mesh):
+    body = fused_device if fits(mesh) else per_device
     in_specs = (
         P(("groups", "row"), "col"),
         P(("groups", "col"), "row"),
@@ -49,5 +368,5 @@
     )
     out_specs = (P(("groups", "col"), "row"), P(("groups", "row"), "col"))
     return jax.shard_map(
-        per_device, mesh=mesh, in_specs=in_specs, out_specs=out_specs, check_vma=False
-    )
+        body, mesh=mesh, in_specs=in_specs, out_specs=out_specs, check_vma=False
+    )

time: 285 us -> 255 us (0.89)
  Pallas kernels: 0 us -> 213 us
  waiting for transfers between devices: 198 us -> 0.04 us
  matrix products: 59.7 us -> 11.3 us
  local copies, waits for them, and re-layouts: 0.01 us -> 3.46 us
    pallas_call x0 -> x1, Pallas kernels: none -> 213 us  [gathered_product(): pl.pallas_call(kernel, out_shape=(jax.ShapeDtypeStruct((tokens, hidden),...]
    all_gather x1 -> x0, waiting for transfers between devices: 113 us -> none  [per_device(): grad_rows = lax.all_gather(grad_out, 'row', axis=0, tiled=True)]
    reduce_scatter x2 -> x0, waiting for transfers between devices: 84.1 us -> none  [the longest x1 84.1 us: per_device(): lax.psum_scatter(lax.dot_general(grad_rows, down_weight, (((1,), (1,)), (...]
    dot_general x3 -> x2, matrix products: 59.7 us -> 11.3 us  [the longest x1 6.21 us: fused_device(): lax.dot_general(sketch_matrix, value.astype(jnp.bfloat16), (((0,), (1,)),...]
    unnamed x2 -> x7, local copies, waits for them, and re-layouts: 0.01 us -> 3.46 us
    convert_element_type x2 -> x1, other arithmetic: 7.84 us -> 5.14 us  [fused_device(): slope.astype(jnp.bfloat16)]
  transfers between devices with their start and end apart: 3 -> 1, of which waited for: 2 -> 0; matrix products, arithmetic and copies ran while one was open for 21% -> 2% of each run, Pallas kernels for 0% -> 84%
where the time goes in v2:
time: 255 us
  Pallas kernels  213 us (84%)
  between operations  14.1 us (6%)
  matrix products  11.3 us (4%)
  blocking collectives  7.85 us (3%)
  other arithmetic  5.14 us (2%)
  local copies, waits for them, and re-layouts  3.46 us (1%)
    pallas_call x1, Pallas kernels, gathered_product(): pl.pallas_call(kernel, out_shape=(jax.ShapeDtypeStruct((tokens, hidden),...  213 us
    all_gather x1, blocking collectives, fused_device(): lax.all_gather(reduced.astype(jnp.bfloat16), 'col', axis=1, tiled=True)  7.85 us
    dot_general x1, matrix products, fused_device(): lax.dot_general(sketch_matrix, value.astype(jnp.bfloat16), (((0,), (1,)),...  6.21 us
    convert_element_type x1, other arithmetic, fused_device(): slope.astype(jnp.bfloat16)  5.14 us
    dot_general x1, matrix products, fused_device(): sketch = jnp.dot(reduced, grad_rows, preferred_element_type=jnp.float32)  5.1 us
  transfers between devices with their start and end apart: 1, of which 0 were waited for; matrix products, arithmetic and copies ran while one was open for 2% of the time, Pallas kernels for 84%

profile of v2, /device:TPU:0, one launch (start us, length us, event | category | flops | bytes accessed | tf_op | source)
XLA Modules:
  0.0 254.9 jit_solution(5891552472025951214)
XLA Ops:
  7.2 0.0 copy-start
  7.2 0.0 reduce-scatter.4.cloned.1.call-start
  7.2 6.2 %fusion.15 = bf16[512,256]{0,1:T(8,128)(2,1)S(1)} fusion(bf16[6144,512]{1,0:T(8,128)(2,1)} %param.7, bf16[256,6144]{1,0:T(8,128)(2,1)} %param.5), kind=kOutput, calls=%fused_computation.19 | convolution fusion | flops 1626472448 | bytes 9699328 | tf_op jit(solution)/shard_map/dot_general | solution.py:352
  13.4 0.8 copy.6
  14.3 0.0 reduce-scatter.4.cloned.1.call-update
  14.3 0.0 copy-done
  14.3 5.1 %fusion.5.slope_ref = bf16[256,6144]{1,0:T(8,128)(2,1)} fusion(bf16[256,6144]{1,0:T(8,128)(2,1)S(1)} %copy-done), kind=kLoop, calls=%fused_computation.12 | loop fusion | flops 29884416 | bytes 6291456 | tf_op jit(solution)/shard_map/convert_element_type | solution.py:351
  19.5 213.0 %shard_map.59 = (bf16[256,6144]{1,0:T(8,128)(2,1)}, bf16[1024,3072]{1,0:T(8,128)(2,1)}) custom-call(bf16[256,3072]{1,0:T(8,128)(2,1)} %g_ref.1, bf16[6144,3072]{1,0:T(8,128)(2,1)} %w_ref.1, bf16[256,6144]{1,0:T(8,128)(2,1)} %fusion.5.slope_ref), custom_call_target="tpu_custom_call" | custom-call | flops 115964116992 | bytes 56623104 | tf_op jit(solution)/shard_map/pallas_call | solution.py:318
  232.5 0.0 reduce-scatter.4.cloned.1.call-done
  232.5 0.9 copy.7
  233.5 7.8 %all_gather.3 = bf16[128,1024]{0,1:T(8,128)(2,1)S(1)} all-gather(bf16[128,256]{0,1:T(8,128)(2,1)S(1)} %copy.7), channel_id=1, replica_groups=mesh['groups'=2,'row'=4,'col'=4] {'col'}, dimensions={1}, use_global_device_ids=true | all-gather | bytes 327680 | tf_op jit(solution)/shard_map/all_gather | solution.py:356
  241.3 0.0 copy-start.1
  241.3 5.1 %fusion.22 = f32[128,3072]{1,0:T(8,128)} fusion(bf16[128,1024]{0,1:T(8,128)(2,1)S(1)} %all_gather.3, bf16[1024,3072]{1,0:T(8,128)(2,1)} %get-tuple-element.5), kind=kOutput, calls=%fused_computation.24 | convolution fusion | flops 805306368 | bytes 8126464 | tf_op jit(solution)/shard_map/dot_general | solution.py:357
  246.4 0.0 copy-done.1
  246.4 1.7 copy.9
Async XLA Ops:
  7.2 7.1 %copy-start = (bf16[256,6144]{1,0:T(8,128)(2,1)S(1)}, bf16[256,6144]{1,0:T(8,128)(2,1)}, u32[]{:S(2)}) copy-start(bf16[256,6144]{1,0:T(8,128)(2,1)} %param.5) | copy-start | bytes 9437188
  7.2 225.3 %reduce-scatter.4.cloned.1.call-start = ((), (), s32[]{:S(2)}) async-start(), calls=%async_computation.1 | async-start | bytes 327680
  241.3 5.1 %copy-start.1 = (bf16[256,6144]{1,0:T(8,128)(2,1)S(1)}, bf16[256,6144]{1,0:T(8,128)(2,1)}, u32[]{:S(2)}) copy-start(bf16[256,6144]{1,0:T(8,128)(2,1)} %get-tuple-element.8) | copy-start | bytes 9437188
Sparse Core Ops, SparseCore 0:
  14.4 23.8 reduce-scatter.3

commit v3 on v2

--- a/solution.py
+++ b/solution.py
@@ -44,7 +44,7 @@
 
 MESH = pl.DeviceIdType.MESH
 LINE = 4
-TILES = 6
+TILES = 3
 
 
 def fits(mesh):
@@ -58,29 +58,17 @@
     return chosen
 
 
-def encoded(pieces):
-    code = 0
-    for piece in reversed(pieces):
-        code = code * 8 + piece
-    return code
-
-
 def arrival_orders():
-    orders = []
+    codes = []
     for place in range(LINE):
-        order = [2 * place, 2 * place + 1]
-        for distance in range(1, LINE):
-            for half in range(2):
-                for other in (place - distance, place + distance):
-                    if 0 <= other < LINE:
-                        order.append(2 * other + half)
-        orders.append(encoded(order))
-    return orders
+        order = sorted(range(LINE), key=lambda block: (abs(block - place), block))
+        codes.append(sum(block * LINE**position for position, block in enumerate(order)))
+    return codes
 
 
 def kernel(
     g_ref, w_ref, slope_ref, out_ref, rows_ref,
-    wbuf, gbuf, pbuf, near, far, sums, slopes,
+    wbuf, gbuf, pbuf, near, far, sums,
     w_sem, g_sem, own_sem, slope_sem, out_sem, right_sem, left_sem, got_sem,
     near_send, near_got, far_send, far_got, sum_send, sum_got,
 ):
@@ -91,7 +79,7 @@
     partner = c + 1 - 2 * par
     chip = lax.div(c, 2)
     has_left, has_right = z > 0, z < LINE - 1
-    piece_rows = gbuf.shape[0]
+    piece_rows = gbuf.shape[0] // 2
     tile = wbuf.shape[2]
     half_width = tile * TILES
 
@@ -102,7 +90,7 @@
     def slope_copy(h, half):
         return pltpu.make_async_copy(
             slope_ref.at[pl.ds(h * piece_rows, piece_rows), pl.ds(half * half_width, half_width)],
-            slopes.at[h, half],
+            far.at[2 * h + half],
             slope_sem.at[h, half],
         )
 
@@ -183,32 +171,40 @@
     def _(j):
         w_copy(par, j).start()
 
-    for h in range(2):
-        for half in range(2):
-            slope_copy(h, half).start()
     own_copy().wait()
 
+    def receive(block):
+        for h in range(2):
+            piece = 2 * block + h
+            pass_on(piece, 0, left_sem, rows_of(piece)).wait_recv()
+
+            @pl.when((block < z) & has_right)
+            def _():
+                pass_on(piece, 1, right_sem, rows_of(piece)).start()
+
+            @pl.when((block > z) & has_left)
+            def _():
+                pass_on(piece, -1, left_sem, rows_of(piece)).start()
+
+    middle = has_left & has_right
+
     def step_of(s, code):
-        piece = lax.rem(code, 8)
-        owner = lax.div(piece, 2)
-        h = lax.rem(piece, 2)
+        owner = lax.rem(code, LINE)
+        later = lax.rem(lax.div(code, LINE), LINE)
         is_near = owner == partner
         is_far = lax.div(owner, 2) != chip
-        index = 2 * lax.rem(owner, 2) + h
-
-        @pl.when(owner != z)
-        def _():
-            pass_on(piece, 0, left_sem, rows_of(piece)).wait_recv()
-
-        @pl.when((owner < z) & has_right)
-        def _():
-            pass_on(piece, 1, right_sem, rows_of(piece)).start()
-
-        @pl.when((owner > z) & has_left)
-        def _():
-            pass_on(piece, -1, left_sem, rows_of(piece)).start()
-
-        load = pltpu.make_async_copy(rows_of(piece), gbuf, g_sem)
+        first = 2 * lax.rem(owner, 2)
+
+        @pl.when((s > 0) & ((s != 2) | jnp.logical_not(middle)))
+        def _():
+            receive(owner)
+
+        @pl.when((s == 1) & middle)
+        def _():
+            receive(later)
+
+        start = pl.multiple_of(owner * 2 * piece_rows, 2 * piece_rows)
+        load = pltpu.make_async_copy(rows_ref.at[pl.ds(start, 2 * piece_rows)], gbuf, g_sem)
         load.start()
         load.wait()
 
@@ -221,40 +217,53 @@
 
                 product = lax.dot_general(
                     gbuf[...], wbuf[half, j], (((1,), (1,)), ((), ())), preferred_element_type=jnp.float32
-                )
-                pbuf[piece, half, :, pl.ds(pl.multiple_of(j * tile, tile), tile)] = product.astype(jnp.bfloat16)
+                ).astype(jnp.bfloat16)
+                columns = pl.ds(pl.multiple_of(j * tile, tile), tile)
+                for h in range(2):
+                    pbuf[2 * owner + h, half, :, columns] = product[h * piece_rows : (h + 1) * piece_rows]
 
         multiply(other)
 
         @pl.when(is_near)
         def _():
-            near_copy(piece, h, other).start()
+            for h in range(2):
+                near_copy(2 * owner + h, h, other).start()
 
         @pl.when(is_far)
         def _():
-            far_copy(piece, index).start()
+            for h in range(2):
+                far_copy(2 * owner + h, first + h).start()
 
         multiply(par)
 
         @pl.when(is_near)
         def _():
-            near_copy(piece, h, par).start()
+            for h in range(2):
+                near_copy(2 * owner + h, h, par).start()
 
         @pl.when(is_far)
         def _():
-            far_copy(piece, index).wait_recv()
-
-            @pl.loop(0, TILES)
-            def _(j):
-                columns = pl.ds(pl.multiple_of(j * tile, tile), tile)
-                total = pbuf[piece, par, :, columns].astype(jnp.float32) + far[index, :, columns].astype(jnp.float32)
-                pbuf[piece, par, :, columns] = total.astype(jnp.bfloat16)
-
-            sum_copy(piece, owner, h, par, index).start()
-
-        return lax.div(code, 8)
-
-    lax.fori_loop(0, 2 * LINE, step_of, pick(z, arrival_orders()))
+            for h in range(2):
+                piece, index = 2 * owner + h, first + h
+                far_copy(piece, index).wait_recv()
+
+                @pl.loop(0, TILES)
+                def _(j):
+                    columns = pl.ds(pl.multiple_of(j * tile, tile), tile)
+                    total = pbuf[piece, par, :, columns].astype(jnp.float32) + far[index, :, columns].astype(
+                        jnp.float32
+                    )
+                    pbuf[piece, par, :, columns] = total.astype(jnp.bfloat16)
+
+                sum_copy(piece, owner, h, par, index).start()
+
+        return lax.div(code, LINE)
+
+    lax.fori_loop(0, LINE, step_of, pick(z, arrival_orders()))
+
+    for h in range(2):
+        for half in range(2):
+            slope_copy(h, half).start()
 
     for h in range(2):
         for half in range(2):
@@ -270,7 +279,7 @@
                     + near[h, half, :, columns].astype(jnp.float32)
                     + sums[h, half, :, columns].astype(jnp.float32)
                 )
-                scaled = hidden * slopes[h, half, :, columns].astype(jnp.float32)
+                scaled = hidden * far[2 * h + half, :, columns].astype(jnp.float32)
                 pbuf[2 * c + h, half, :, columns] = scaled.astype(jnp.bfloat16)
 
             out_copy(h, half).start()
@@ -325,11 +334,10 @@
         out_specs=(pl.BlockSpec(memory_space=pltpu.HBM),) * 2,
         scratch_shapes=[
             pltpu.VMEM((2, TILES, width // TILES, features), kind),
-            pltpu.VMEM((rows, features), kind),
+            pltpu.VMEM((2 * rows, features), kind),
             pltpu.VMEM((2 * LINE, 2, rows, width), kind),
             pltpu.VMEM((2, 2, rows, width), kind),
             pltpu.VMEM((4, rows, width), kind),
-            pltpu.VMEM((2, 2, rows, width), kind),
             pltpu.VMEM((2, 2, rows, width), kind),
             pltpu.SemaphoreType.DMA((2, TILES)),
             one, one, pair, pair, eight, eight, eight,

time: 255 us -> 221 us (0.87)
  Pallas kernels: 213 us -> 179 us
    pallas_call x1, Pallas kernels: 213 us -> 179 us  [gathered_product(): pl.pallas_call(kernel, out_shape=(jax.ShapeDtypeStruct((tokens, hidden),...]
  transfers between devices with their start and end apart: 1 -> 1, of which waited for: 0 -> 0; matrix products, arithmetic and copies ran while one was open for 2% -> 2% of each run, Pallas kernels for 84% -> 81%
where the time goes in v3:
time: 221 us
  Pallas kernels  179 us (81%)
  between operations  14.1 us (6%)
  matrix products  11.3 us (5%)
  blocking collectives  7.81 us (4%)
  other arithmetic  5.14 us (2%)
  local copies, waits for them, and re-layouts  3.46 us (2%)
    pallas_call x1, Pallas kernels, gathered_product(): pl.pallas_call(kernel, out_shape=(jax.ShapeDtypeStruct((tokens, hidden),...  179 us
    all_gather x1, blocking collectives, fused_device(): lax.all_gather(reduced.astype(jnp.bfloat16), 'col', axis=1, tiled=True)  7.81 us
    dot_general x1, matrix products, fused_device(): lax.dot_general(sketch_matrix, value.astype(jnp.bfloat16), (((0,), (1,)),...  6.21 us
    convert_element_type x1, other arithmetic, fused_device(): slope.astype(jnp.bfloat16)  5.14 us
    dot_general x1, matrix products, fused_device(): sketch = jnp.dot(reduced, grad_rows, preferred_element_type=jnp.float32)  5.11 us
  transfers between devices with their start and end apart: 1, of which 0 were waited for; matrix products, arithmetic and copies ran while one was open for 2% of the time, Pallas kernels for 81%

profile of v3, /device:TPU:0, one launch (start us, length us, event | category | flops | bytes accessed | tf_op | source)
XLA Modules:
  0.0 221.1 jit_solution(6869269341790006507)
XLA Ops:
  7.2 0.0 copy-start
  7.2 0.0 reduce-scatter.4.cloned.1.call-start
  7.2 6.2 %fusion.15 = bf16[512,256]{0,1:T(8,128)(2,1)S(1)} fusion(bf16[6144,512]{1,0:T(8,128)(2,1)} %param.7, bf16[256,6144]{1,0:T(8,128)(2,1)} %param.5), kind=kOutput, calls=%fused_computation.19 | convolution fusion | flops 1626472448 | bytes 9699328 | tf_op jit(solution)/shard_map/dot_general | solution.py:360
  13.4 0.8 copy.6
  14.3 0.0 reduce-scatter.4.cloned.1.call-update
  14.3 0.0 copy-done
  14.3 5.1 %fusion.5.slope_ref = bf16[256,6144]{1,0:T(8,128)(2,1)} fusion(bf16[256,6144]{1,0:T(8,128)(2,1)S(1)} %copy-done), kind=kLoop, calls=%fused_computation.12 | loop fusion | flops 29884416 | bytes 6291456 | tf_op jit(solution)/shard_map/convert_element_type | solution.py:359
  19.5 179.3 %shard_map.59 = (bf16[256,6144]{1,0:T(8,128)(2,1)}, bf16[1024,3072]{1,0:T(8,128)(2,1)}) custom-call(bf16[256,3072]{1,0:T(8,128)(2,1)} %g_ref.1, bf16[6144,3072]{1,0:T(8,128)(2,1)} %w_ref.1, bf16[256,6144]{1,0:T(8,128)(2,1)} %fusion.5.slope_ref), custom_call_target="tpu_custom_call" | custom-call | flops 115964116992 | bytes 56623104 | tf_op jit(solution)/shard_map/pallas_call | solution.py:327
  198.7 0.0 reduce-scatter.4.cloned.1.call-done
  198.8 0.9 copy.7
  199.7 7.8 %all_gather.3 = bf16[128,1024]{0,1:T(8,128)(2,1)S(1)} all-gather(bf16[128,256]{0,1:T(8,128)(2,1)S(1)} %copy.7), channel_id=1, replica_groups=mesh['groups'=2,'row'=4,'col'=4] {'col'}, dimensions={1}, use_global_device_ids=true | all-gather | bytes 327680 | tf_op jit(solution)/shard_map/all_gather | solution.py:364
  207.5 0.0 copy-start.1
  207.5 5.1 %fusion.22 = f32[128,3072]{1,0:T(8,128)} fusion(bf16[128,1024]{0,1:T(8,128)(2,1)S(1)} %all_gather.3, bf16[1024,3072]{1,0:T(8,128)(2,1)} %get-tuple-element.5), kind=kOutput, calls=%fused_computation.24 | convolution fusion | flops 805306368 | bytes 8126464 | tf_op jit(solution)/shard_map/dot_general | solution.py:365
  212.6 0.0 copy-done.1
  212.6 1.7 copy.9
Async XLA Ops:
  7.2 7.1 %copy-start = (bf16[256,6144]{1,0:T(8,128)(2,1)S(1)}, bf16[256,6144]{1,0:T(8,128)(2,1)}, u32[]{:S(2)}) copy-start(bf16[256,6144]{1,0:T(8,128)(2,1)} %param.5) | copy-start | bytes 9437188
  7.2 191.6 %reduce-scatter.4.cloned.1.call-start = ((), (), s32[]{:S(2)}) async-start(), calls=%async_computation.1 | async-start | bytes 327680
  207.5 5.1 %copy-start.1 = (bf16[256,6144]{1,0:T(8,128)(2,1)S(1)}, bf16[256,6144]{1,0:T(8,128)(2,1)}, u32[]{:S(2)}) copy-start(bf16[256,6144]{1,0:T(8,128)(2,1)} %get-tuple-element.8) | copy-start | bytes 9437188
Sparse Core Ops, SparseCore 0:
  14.4 23.8 reduce-scatter.3

commit v4 on v3

--- a/solution.py
+++ b/solution.py
@@ -44,7 +44,7 @@
 
 MESH = pl.DeviceIdType.MESH
 LINE = 4
-TILES = 3
+TILES = 4
 
 
 def fits(mesh):
@@ -122,17 +122,20 @@
             device_id={"col": partner}, device_id_type=MESH,
         )
 
-    def far_copy(piece, index):
+    def part(q):
+        return pl.ds(q * (half_width // 2), half_width // 2)
+
+    def far_copy(piece, index, q):
         return pltpu.make_async_remote_copy(
-            src_ref=pbuf.at[piece, other], dst_ref=far.at[index],
-            send_sem=far_send.at[index], recv_sem=far_got.at[index],
+            src_ref=pbuf.at[piece, other, :, part(q)], dst_ref=far.at[index, :, part(q)],
+            send_sem=far_send.at[index, q], recv_sem=far_got.at[index, q],
             device_id={"col": partner}, device_id_type=MESH,
         )
 
-    def sum_copy(piece, owner, h, half, index):
+    def sum_copy(piece, owner, h, half, index, q):
         return pltpu.make_async_remote_copy(
-            src_ref=pbuf.at[piece, half], dst_ref=sums.at[h, half],
-            send_sem=sum_send.at[index], recv_sem=sum_got.at[h, half],
+            src_ref=pbuf.at[piece, half, :, part(q)], dst_ref=sums.at[h, half, :, part(q)],
+            send_sem=sum_send.at[index, q], recv_sem=sum_got.at[h, half, q],
             device_id={"col": owner}, device_id_type=MESH,
         )
 
@@ -208,8 +211,8 @@
         load.start()
         load.wait()
 
-        def multiply(half):
-            @pl.loop(0, TILES)
+        def multiply(half, q):
+            @pl.loop(q * (TILES // 2), (q + 1) * (TILES // 2))
             def _(j):
                 @pl.when(s == 0)
                 def _():
@@ -222,40 +225,37 @@
                 for h in range(2):
                     pbuf[2 * owner + h, half, :, columns] = product[h * piece_rows : (h + 1) * piece_rows]
 
-        multiply(other)
+        for q in range(2):
+            multiply(other, q)
+
+            @pl.when(is_far)
+            def _():
+                for h in range(2):
+                    far_copy(2 * owner + h, first + h, q).start()
+
+            multiply(par, q)
+
+            @pl.when(is_far)
+            def _():
+                for h in range(2):
+                    piece, index = 2 * owner + h, first + h
+                    far_copy(piece, index, q).wait_recv()
+
+                    @pl.loop(q * (TILES // 2), (q + 1) * (TILES // 2))
+                    def _(j):
+                        columns = pl.ds(pl.multiple_of(j * tile, tile), tile)
+                        total = pbuf[piece, par, :, columns].astype(jnp.float32) + far[index, :, columns].astype(
+                            jnp.float32
+                        )
+                        pbuf[piece, par, :, columns] = total.astype(jnp.bfloat16)
+
+                    sum_copy(piece, owner, h, par, index, q).start()
 
         @pl.when(is_near)
         def _():
-            for h in range(2):
-                near_copy(2 * owner + h, h, other).start()
-
-        @pl.when(is_far)
-        def _():
-            for h in range(2):
-                far_copy(2 * owner + h, first + h).start()
-
-        multiply(par)
-
-        @pl.when(is_near)
-        def _():
-            for h in range(2):
-                near_copy(2 * owner + h, h, par).start()
-
-        @pl.when(is_far)
-        def _():
-            for h in range(2):
-                piece, index = 2 * owner + h, first + h
-                far_copy(piece, index).wait_recv()
-
-                @pl.loop(0, TILES)
-                def _(j):
-                    columns = pl.ds(pl.multiple_of(j * tile, tile), tile)
-                    total = pbuf[piece, par, :, columns].astype(jnp.float32) + far[index, :, columns].astype(
-                        jnp.float32
-                    )
-                    pbuf[piece, par, :, columns] = total.astype(jnp.bfloat16)
-
-                sum_copy(piece, owner, h, par, index).start()
+            for half in range(2):
+                for h in range(2):
+                    near_copy(2 * owner + h, h, half).start()
 
         return lax.div(code, LINE)
 
@@ -269,7 +269,8 @@
         for half in range(2):
             near_copy(2 * partner + h, h, half).wait_recv()
             slope_copy(h, half).wait()
-            sum_copy(2 * c + h, lax.rem(c + 2, LINE), h, half, h).wait_recv()
+            for q in range(2):
+                sum_copy(2 * c + h, lax.rem(c + 2, LINE), h, half, h, q).wait_recv()
 
             @pl.loop(0, TILES)
             def _(j):
@@ -304,8 +305,9 @@
 
         @pl.when(lax.div(owner, 2) != chip)
         def _():
-            far_copy(piece, index).wait_send()
-            sum_copy(piece, owner, h, par, index).wait_send()
+            for q in range(2):
+                far_copy(piece, index, q).wait_send()
+                sum_copy(piece, owner, h, par, index, q).wait_send()
 
         return carry
 
@@ -322,7 +324,7 @@
     kind = grad_out.dtype
     pair = pltpu.SemaphoreType.DMA((2, 2))
     eight = pltpu.SemaphoreType.DMA((2 * LINE,))
-    four = pltpu.SemaphoreType.DMA((4,))
+    four = pltpu.SemaphoreType.DMA((4, 2))
     one = pltpu.SemaphoreType.DMA
     return pl.pallas_call(
         kernel,
@@ -341,7 +343,7 @@
             pltpu.VMEM((2, 2, rows, width), kind),
             pltpu.SemaphoreType.DMA((2, TILES)),
             one, one, pair, pair, eight, eight, eight,
-            pair, pair, four, four, four, pair,
+            pair, pair, four, four, four, pltpu.SemaphoreType.DMA((2, 2, 2)),
         ],
         compiler_params=pltpu.CompilerParams(
             collective_id=0, has_side_effects=True, vmem_limit_bytes=63 * 1024 * 1024

time: 221 us -> 217 us (0.982)
  Pallas kernels: 179 us -> 175 us
    pallas_call x1, Pallas kernels: 179 us -> 175 us  [gathered_product(): pl.pallas_call(kernel, out_shape=(jax.ShapeDtypeStruct((tokens, hidden),...]
where the time goes in v4:
time: 217 us
  Pallas kernels  175 us (81%)
  between operations  14.1 us (6%)
  matrix products  11.3 us (5%)
  blocking collectives  7.83 us (4%)
  other arithmetic  5.14 us (2%)
  local copies, waits for them, and re-layouts  3.46 us (2%)
    pallas_call x1, Pallas kernels, gathered_product(): pl.pallas_call(kernel, out_shape=(jax.ShapeDtypeStruct((tokens, hidden),...  175 us
    all_gather x1, blocking collectives, fused_device(): lax.all_gather(reduced.astype(jnp.bfloat16), 'col', axis=1, tiled=True)  7.83 us
    dot_general x1, matrix products, fused_device(): lax.dot_general(sketch_matrix, value.astype(jnp.bfloat16), (((0,), (1,)),...  6.21 us
    convert_element_type x1, other arithmetic, fused_device(): slope.astype(jnp.bfloat16)  5.14 us
    dot_general x1, matrix products, fused_device(): sketch = jnp.dot(reduced, grad_rows, preferred_element_type=jnp.float32)  5.11 us
  transfers between devices with their start and end apart: 1, of which 0 were waited for; matrix products, arithmetic and copies ran while one was open for 2% of the time, Pallas kernels for 81%

profile of v4, /device:TPU:0, one launch (start us, length us, event | category | flops | bytes accessed | tf_op | source)
XLA Modules:
  0.0 216.8 jit_solution(17854295860152656039)
XLA Ops:
  7.2 0.0 copy-start
  7.2 0.0 reduce-scatter.4.cloned.1.call-start
  7.2 6.2 %fusion.15 = bf16[512,256]{0,1:T(8,128)(2,1)S(1)} fusion(bf16[6144,512]{1,0:T(8,128)(2,1)} %param.7, bf16[256,6144]{1,0:T(8,128)(2,1)} %param.5), kind=kOutput, calls=%fused_computation.19 | convolution fusion | flops 1626472448 | bytes 9699328 | tf_op jit(solution)/shard_map/dot_general | solution.py:362
  13.4 0.8 copy.6
  14.3 0.0 reduce-scatter.4.cloned.1.call-update
  14.3 0.0 copy-done
  14.3 5.1 %fusion.5.slope_ref = bf16[256,6144]{1,0:T(8,128)(2,1)} fusion(bf16[256,6144]{1,0:T(8,128)(2,1)S(1)} %copy-done), kind=kLoop, calls=%fused_computation.12 | loop fusion | flops 29884416 | bytes 6291456 | tf_op jit(solution)/shard_map/convert_element_type | solution.py:361
  19.5 174.9 %shard_map.59 = (bf16[256,6144]{1,0:T(8,128)(2,1)}, bf16[1024,3072]{1,0:T(8,128)(2,1)}) custom-call(bf16[256,3072]{1,0:T(8,128)(2,1)} %g_ref.1, bf16[6144,3072]{1,0:T(8,128)(2,1)} %w_ref.1, bf16[256,6144]{1,0:T(8,128)(2,1)} %fusion.5.slope_ref), custom_call_target="tpu_custom_call" | custom-call | flops 115964116992 | bytes 56623104 | tf_op jit(solution)/shard_map/pallas_call | solution.py:329
  194.3 0.0 reduce-scatter.4.cloned.1.call-done
  194.4 0.9 copy.7
  195.3 7.8 %all_gather.3 = bf16[128,1024]{0,1:T(8,128)(2,1)S(1)} all-gather(bf16[128,256]{0,1:T(8,128)(2,1)S(1)} %copy.7), channel_id=1, replica_groups=mesh['groups'=2,'row'=4,'col'=4] {'col'}, dimensions={1}, use_global_device_ids=true | all-gather | bytes 327680 | tf_op jit(solution)/shard_map/all_gather | solution.py:366
  203.1 0.0 copy-start.1
  203.1 5.1 %fusion.22 = f32[128,3072]{1,0:T(8,128)} fusion(bf16[128,1024]{0,1:T(8,128)(2,1)S(1)} %all_gather.3, bf16[1024,3072]{1,0:T(8,128)(2,1)} %get-tuple-element.5), kind=kOutput, calls=%fused_computation.24 | convolution fusion | flops 805306368 | bytes 8126464 | tf_op jit(solution)/shard_map/dot_general | solution.py:367
  208.3 0.0 copy-done.1
  208.3 1.7 copy.9
Async XLA Ops:
  7.2 7.1 %copy-start = (bf16[256,6144]{1,0:T(8,128)(2,1)S(1)}, bf16[256,6144]{1,0:T(8,128)(2,1)}, u32[]{:S(2)}) copy-start(bf16[256,6144]{1,0:T(8,128)(2,1)} %param.5) | copy-start | bytes 9437188
  7.2 187.2 %reduce-scatter.4.cloned.1.call-start = ((), (), s32[]{:S(2)}) async-start(), calls=%async_computation.1 | async-start | bytes 327680
  203.1 5.1 %copy-start.1 = (bf16[256,6144]{1,0:T(8,128)(2,1)S(1)}, bf16[256,6144]{1,0:T(8,128)(2,1)}, u32[]{:S(2)}) copy-start(bf16[256,6144]{1,0:T(8,128)(2,1)} %get-tuple-element.8) | copy-start | bytes 9437188
Sparse Core Ops, SparseCore 0:
  14.4 23.8 reduce-scatter.3
